TPU v7x, 256 devices: a whole 4x4x8 slice. The times are simulated.
256 devices in a mesh: stream: 32 (over x, z), azim: 8 (over y, core).
Axes of the slice: x: 4, y: 4, z: 8, core: 2. Of those that a mesh axis runs over, the one named last changes fastest.
Arguments:
- species_mass_density: float32 [14, 256, 32, 1024], P(None, 'stream', None, 'azim'), may hold values from -6 to 6
- axial_speed: float32 [256, 32, 1024], P('stream', None, 'azim'), may hold values from -6 to 6
- circumferential_speed: float32 [256, 32, 1024], P('stream', None, 'azim'), may hold values from -6 to 6
- thermal_kelvin_field: float32 [256, 32, 1024], P('stream', None, 'azim'), may hold values from 1 to 4
- arrhenius_multiplier: float32 [32], replicated, may hold values from 0.8 to 810
- arrhenius_threshold: float32 [32], replicated, may hold values from 2 to 24
- consumed_species_orders: float32 [32, 14], replicated, may hold values from -1.5 to 1.5
- net_molar_change: float32 [14, 32], replicated, may hold values from -1 to 1
- ablated_mixture_table: float32 [14, 14], replicated, may hold values from -1.5 to 1.5
- ablator_boundary_condition: float32 [8192, 14, 1024], P('stream', None, 'azim'), may hold values from -6 to 6
- holding_segment: int32 [8192], P('stream'), may hold values from 0 to 31, as said below
- intra_segment_position: int32 [8192], P('stream'), may hold values from 0 to 7
- shocked_level_bounds: int32 [32, 2], P('stream'), may hold values from 0 to 32, as said below
Outputs:
- rhs: float32 [14, 256, 32, 1024], P(None, 'stream', None, 'azim')
Inputs may be any that keep to these rules, and one draw needn't show every extreme that they name: `holding_segment`: in each aligned block of 256 entries no tile appears more than 16 times, and some tile appears exactly 16 times in every block. Each row holds 0 <= shocked_level_bounds[t, 0] < shocked_level_bounds[t, 1] <= 32 with shocked_level_bounds[t, 1] - shocked_level_bounds[t, 0] <= 8; some row has exactly 8.
All inputs are finite; a program needn't handle non-finite values.
Results may differ from a plain program's by a relative error of at most 0.0003.
Values sent between devices are 32-bit elements; how exact they have to be, the bound alone decides.
A program may use at most 128 MiB of HBM per device.

v0:
```python
import math

import jax
import jax.numpy as jnp
from jax import lax
from jax.sharding import PartitionSpec as P

STENCIL = (-1.0 / 60.0, 3.0 / 20.0, -0.75, 0.0, 0.75, -3.0 / 20.0, 1.0 / 60.0)
HIGH = lax.Precision.HIGHEST


def padded_2(x, sides, width):
    for axis, dim in sides:
        size, length = (lax.axis_size(axis), x.shape[dim])
        up = [(i, (i + 1) % size) for i in range(size - 1)]
        down = [(j, i) for i, j in up]
        last = lax.slice_in_dim(x, length - width, length, axis=dim)
        first = lax.slice_in_dim(x, 0, width, axis=dim)
        before = lax.ppermute(last, axis, up)
        after = lax.ppermute(first, axis, down)
        x = jnp.concatenate([before, x, after], axis=dim)
    return x


def mode_gains(modes, points):
    wave_int = jnp.arange(modes)
    wave = wave_int.astype(jnp.float32)
    sigma = (3 * wave_int < 2 * modes).astype(jnp.float32)
    return 2.0 * wave * sigma / (points * modes)


def angle_tables(point_index, modes, points):
    wave = jnp.arange(modes)
    product = point_index[:, None] * wave[None, :] % points
    theta = product.astype(jnp.float32) * (2.0 * math.pi / points)
    return (jnp.cos(theta), jnp.sin(theta))


def local(
    species_mass_density,
    axial_speed,
    circumferential_speed,
    thermal_kelvin_field,
    arrhenius_multiplier,
    arrhenius_threshold,
    consumed_species_orders,
    net_molar_change,
    ablated_mixture_table,
    ablator_boundary_condition,
    holding_segment,
    intra_segment_position,
    shocked_level_bounds,
):
    species, cells, rows, local_points = species_mass_density.shape
    groups = lax.axis_size("azim")
    points = local_points * groups
    modes = points // 2
    padded = padded_2(species_mass_density, (("stream", 1),), 3)
    stream_grad = STENCIL[0] * padded[:, 0:cells]
    for offset in range(1, 7):
        if STENCIL[offset] != 0.0:
            stream_grad = stream_grad + STENCIL[offset] * padded[:, offset : offset + cells]
    low_row = shocked_level_bounds[0, 0]
    high_row = shocked_level_bounds[0, 1]
    row_index = jnp.arange(rows)
    in_band = ((row_index >= low_row) & (row_index < high_row)).astype(jnp.float32)
    gains = mode_gains(modes, points)
    all_index = jnp.arange(points)
    cos_all, sin_all = angle_tables(all_index, modes, points)
    forward = jnp.concatenate([cos_all, sin_all], axis=1)
    inverse = jnp.concatenate([-(gains[:, None] * sin_all.T), gains[:, None] * cos_all.T], axis=0)
    block = lax.all_to_all(species_mass_density, "azim", split_axis=1, concat_axis=3, tiled=True)
    flat = block.reshape(-1, points)
    spectrum = jnp.dot(flat, forward, precision=HIGH, preferred_element_type=jnp.float32)
    values = jnp.dot(spectrum, inverse, precision=HIGH, preferred_element_type=jnp.float32).reshape(
        block.shape
    )
    azim_grad = lax.all_to_all(values, "azim", split_axis=3, concat_axis=1, tiled=True)
    mixed = jnp.einsum(
        "rs,sxya->rxya", consumed_species_orders, species_mass_density, precision=HIGH
    )
    rate = arrhenius_multiplier[:, None, None, None] * jnp.exp(
        -arrhenius_threshold[:, None, None, None] / thermal_kelvin_field[None]
    )
    chem = jnp.einsum("sr,rxya->sxya", net_molar_change, rate * mixed, precision=HIGH)
    tiles = lax.axis_size("stream")
    elements = holding_segment.shape[0]
    flux = jnp.einsum(
        "st,etj->esj", ablated_mixture_table, ablator_boundary_condition, precision=HIGH
    )
    capacity = 2 * elements // tiles
    member = (holding_segment[:, None] == jnp.arange(tiles)[None, :]).astype(jnp.int32)
    slot = jnp.sum(member * (jnp.cumsum(member, axis=0) - 1), axis=1)
    target = holding_segment * capacity + slot
    placing = (jnp.arange(tiles * capacity)[:, None] == target[None, :]).astype(jnp.float32)
    outgoing = jnp.einsum("pe,esj->psj", placing, flux, precision=HIGH).reshape(
        tiles, capacity, species, local_points
    )
    out_cells = (
        jnp.dot(placing, (intra_segment_position + 1).astype(jnp.float32), precision=HIGH) - 1.0
    ).reshape(tiles, capacity)
    incoming, in_cells = (
        lax.all_to_all(outgoing, "stream", split_axis=0, concat_axis=0, tiled=True),
        lax.all_to_all(out_cells, "stream", split_axis=0, concat_axis=0, tiled=True),
    )
    hits = (in_cells.reshape(-1)[None, :] == jnp.arange(cells).astype(jnp.float32)[:, None]).astype(
        jnp.float32
    )
    wall = jnp.einsum(
        "xq,qsj->sxj",
        hits,
        incoming.reshape(tiles * capacity, species, local_points),
        precision=HIGH,
    )
    rhs = (
        -axial_speed[None] * stream_grad
        - circumferential_speed[None] * in_band[None, None, :, None] * azim_grad
        + chem
    )
    return rhs.at[:, :, 0, :].add(wall)


def solution(mesh):
    in_specs = (
        P(None, "stream", None, "azim"),
        P("stream", None, "azim"),
        P("stream", None, "azim"),
        P("stream", None, "azim"),
        P(),
        P(),
        P(),
        P(),
        P(),
        P("stream", None, "azim"),
        P("stream"),
        P("stream"),
        P("stream", None),
    )
    out_specs = P(None, "stream", None, "azim")
    return jax.shard_map(local, mesh=mesh, in_specs=in_specs, out_specs=out_specs, check_vma=False)
```

profile of v0, /device:TPU:2, one launch (start us, length us, event | category | flops | bytes accessed | tf_op | source)
XLA Modules:
  0.0 345.4 jit_solution(130041774773745954)
XLA Ops:
  0.0 2.9 copy.52
  2.9 4.6 %all-to-all-start = ((f32[14,8,32,128]{3,2,0,1:T(8,128)}), f32[14,8,32,128]{3,2,0,1:T(8,128)}, u32[]{:S(2)}, u32[]{:S(2)}) async-start(f32[14,8,32,128]{3,2,0,1:T(8,128)} %copy.52), calls=%async_computation | async-start | bytes 3670016 | tf_op jit(solution)/shard_map/all_to_all | solution.py:72
  9.6 9.0 %fusion.46 = (f32[1024,512]{1,0:T(8,128)S(1)}, f32[1024,512]{1,0:T(8,128)}) fusion(), kind=kLoop, calls=%fused_computation.61 | loop fusion | flops 7340032 | bytes 4194304 | tf_op jit(solution)/shard_map/sin | solution.py:36
  18.6 9.6 %multiply_negate_fusion = (f32[512,1024]{1,0:T(8,128)}, f32[512,1024]{1,0:T(8,128)}) fusion(f32[512]{0:T(512)S(1)} %fusion.70), kind=kLoop, calls=%fused_computation.49 | loop fusion | flops 8912896 | bytes 4196352 | tf_op jit(solution)/shard_map/neg | solution.py:71
  28.2 3.9 %all-to-all-done = f32[14,8,32,128]{3,2,0,1:T(8,128)} async-done(((f32[14,8,32,128]{3,2,0,1:T(8,128)}), f32[14,8,32,128]{3,2,0,1:T(8,128)}, u32[]{:S(2)}, u32[]{:S(2)}) %all-to-all-start) | async-done | bytes 1835040 | tf_op jit(solution)/shard_map/all_to_all | solution.py:72
  32.0 11.9 %all-to-all-start.3 = ((f32[32,1,16]{2,1,0:T(1,128)}), f32[32,1,16]{2,1,0:T(1,128)S(1)}, u32[]{:S(2)}, u32[]{:S(2)}) async-start(f32[32,1,16]{2,1,0:T(1,128)} %bitcast.22), calls=%async_computation.3 | async-start | bytes 32768 | tf_op jit(solution)/shard_map/all_to_all | solution.py:104
  44.0 3.0 copy.53
  47.0 6.2 %fusion.2 = f32[1024,448]{0,1:T(8,128)S(1)} fusion(f32[1024,512]{1,0:T(8,128)S(1)} %get-tuple-element.25, f32[1024,512]{1,0:T(8,128)S(1)} %copy-done.3, f32[56,8,8,128]{3,2,1,0:T(8,128)S(1)} %bitcast.77), kind=kOutput, calls=%fused_computation.3 | convolution fusion | flops 5638193152 | bytes 7864320 | tf_op jit(solution)/shard_map/dot_general | solution.py:74
  53.2 6.1 %fusion.6 = f32[448,1024]{1,0:T(8,128)S(1)} fusion(f32[1024,448]{0,1:T(8,128)S(1)} %fusion.2, f32[512,1024]{1,0:T(8,128)S(1)} %copy-done.5, f32[512,1024]{1,0:T(8,128)S(1)} %copy-done.4), kind=kOutput, calls=%fused_computation.7 | convolution fusion | flops 5638193152 | bytes 7864320 | tf_op jit(solution)/shard_map/dot_general | solution.py:75
  59.4 12.2 %copy.54 = f32[14,1,32,1024]{2,1,0,3:T(1,128)} copy(f32[14,1,32,1024]{3,2,0,1:T(8,128)S(1)} %bitcast.76) | data formatting | bytes 3670016 | tf_op jit(solution)/shard_map/reshape | solution.py:75
  72.1 66.0 %reduce.8 = f32[1024,14,32]{2,1,0:T(8,128)} reduce(f32[1024,14,1,32]{3,2,1,0:T(1,128)} %bitcast.72, f32[]{:T(128)} %broadcast.143), dimensions={2}, to_apply=%bitcast.66.reduce_sub_computation | reduce | bytes 3670020
  138.1 8.4 %reshape.131 = f32[8,1,57344]{2,1,0:T(1,128)} reshape(f32[1024,14,32]{2,1,0:T(8,128)} %reduce.8) | data formatting | bytes 3670016
  146.6 4.5 %all-to-all-start.1 = ((f32[8,1,57344]{2,1,0:T(1,128)}), f32[8,1,57344]{2,1,0:T(1,128)}, u32[]{:S(2)}, u32[]{:S(2)}) async-start(f32[8,1,57344]{2,1,0:T(1,128)} %reshape.131), calls=%async_computation.1 | async-start | bytes 3670016 | tf_op jit(solution)/shard_map/all_to_all | solution.py:78
  151.1 3.2 fusion.43
  154.3 2.3 fusion.41
  156.6 2.2 copy.61
  158.8 16.6 %all-to-all-done.1 = f32[8,1,57344]{2,1,0:T(1,128)} async-done(((f32[8,1,57344]{2,1,0:T(1,128)}), f32[8,1,57344]{2,1,0:T(1,128)}, u32[]{:S(2)}, u32[]{:S(2)}) %all-to-all-start.1) | async-done | bytes 1835040 | tf_op jit(solution)/shard_map/all_to_all | solution.py:78
  175.4 9.8 %all-to-all-start.2 = ((f32[32,16,14,128]{3,1,2,0:T(8,128)}), f32[32,16,14,128]{3,1,2,0:T(8,128)}, u32[]{:S(2)}, u32[]{:S(2)}) async-start(f32[32,16,14,128]{3,1,2,0:T(8,128)} %copy.61), calls=%async_computation.2 | async-start | bytes 7340032 | tf_op jit(solution)/shard_map/all_to_all | solution.py:103
  186.3 3.4 collective-permute-start
  189.6 4.6 %collective-permute-start.1 = (f32[14,3,32,128]{3,2,1,0:T(8,128)S(1)}, f32[14,3,32,128]{3,2,1,0:T(8,128)S(1)}, u32[]{:S(2)}, u32[]{:S(2)}) collective-permute-start(f32[14,3,32,128]{3,2,1,0:T(8,128)S(1)} %get-tuple-element.20), channel_id=1, source_target_pairs={{8,0},{16,8},{24,16},{32,24},{40,32},{48,40},{56,48},{64,56},{72,6... | collective-permute-start | bytes 2064392 | tf_op jit(solution)/shard_map/ppermute | solution.py:20
  196.3 5.6 %fusion.12 = f32[32,8,32,128]{3,0,2,1:T(8,128)} fusion(f32[14,8,32,128]{3,2,1,0:T(8,128)S(1)} %copy-done.2, f32[32,14]{0,1:T(8,128)S(1)} %copy-done), kind=kOutput, calls=%fused_computation.18 | convolution fusion | flops 176160768 | bytes 6031104 | tf_op jit(solution)/shard_map/rs,sxya->rxya/dot_general | solution.py:79
  203.4 78.0 %collective-permute-done = f32[14,3,32,128]{3,2,1,0:T(8,128)} collective-permute-done((f32[14,3,32,128]{3,2,1,0:T(8,128)}, f32[14,3,32,128]{3,2,1,0:T(8,128)}, u32[]{:S(2)}, u32[]{:S(2)}) %collective-permute-start) | collective-permute-done | bytes 688160 | tf_op jit(solution)/shard_map/ppermute | solution.py:19
  281.4 1.5 copy_dynamic-update-slice_fusion.3
  282.9 2.5 copy_dynamic-update-slice_fusion.1
  285.4 1.6 copy-done.7
  288.3 6.8 %reduce.9 = f32[8,57344]{1,0:T(8,128)S(1)} reduce(f32[8,1,57344]{2,1,0:T(1,128)} %all-to-all-done.1, f32[]{:T(128)} %broadcast.143), dimensions={1}, to_apply=%all_to_all.36.reduce_sub_computation | reduce | bytes 3670020 | tf_op jit(solution)/shard_map/all_to_all | solution.py:78
  295.0 15.7 %reshape.132 = f32[1024,14,1,32]{3,2,1,0:T(1,128)} reshape(f32[8,57344]{1,0:T(8,128)S(1)} %reduce.9) | data formatting | bytes 3670016
  310.8 17.1 %copy.55 = f32[14,1,32,1024]{3,1,2,0:T(1,128)} copy(f32[14,1,32,1024]{2,1,0,3:T(1,128)} %bitcast.73) | data formatting | bytes 3670016 | tf_op jit(solution)/shard_map/all_to_all | solution.py:78
  327.8 11.8 %fusion.23 = f32[14,8,32,128]{3,0,2,1:T(8,128)S(1)} fusion(f32[14,11,32,128]{3,0,2,1:T(8,128)} %copy_dynamic-update-slice_fusion.2, f32[14,11,32,128]{3,0,2,1:T(8,128)} %copy-done.7, f32[14,1,32,8,128]{4,3,1,2,0:T(8,128)} %bitcast.78, f32[8,32,128]{2,1,0:T(8,128)S(1)} %broadcast_multiply_fusion, f32[8,32,128]{2,1,0:T(8,128)S(1)} %neg.11, ...), kind=kOutput, calls=%fused_computation.32 | convolution fusion | flops 186187776 | bytes 19269632 | tf_op jit(solution)/shard_map/sr,rxya->sxya/dot_general | solution.py:85
  339.7 2.4 copy.62
  342.1 1.3 fusion.59
  343.4 1.8 copy.65
  (63 shorter events, 8.3 us)
Async XLA Ops:
  0.0 196.3 %copy-start = (f32[32,14]{0,1:T(8,128)S(1)}, f32[32,14]{0,1:T(8,128)}, u32[]{:S(2)}) copy-start(f32[32,14]{0,1:T(8,128)} %param.21) | copy-start | bytes 5380
  2.9 4.6 %copy-start.10 = (s32[256]{0:T(256)S(1)}, s32[256]{0:T(256)}, u32[]{:S(2)}) copy-start(s32[256]{0:T(256)} %param.25) | copy-start | bytes 3076
  2.9 5.5 %copy-start.13 = (s32[256]{0:T(256)S(1)}, s32[256]{0:T(256)}, u32[]{:S(2)}) copy-start(s32[256]{0:T(256)} %param.26) | copy-start | bytes 3076
  2.9 29.1 %all-to-all-start = ((f32[14,8,32,128]{3,2,0,1:T(8,128)}), f32[14,8,32,128]{3,2,0,1:T(8,128)}, u32[]{:S(2)}, u32[]{:S(2)}) async-start(f32[14,8,32,128]{3,2,0,1:T(8,128)} %copy.52), calls=%async_computation | async-start | bytes 3670016 | tf_op jit(solution)/shard_map/all_to_all | solution.py:72
  32.0 114.5 %all-to-all-start.3 = ((f32[32,1,16]{2,1,0:T(1,128)}), f32[32,1,16]{2,1,0:T(1,128)S(1)}, u32[]{:S(2)}, u32[]{:S(2)}) async-start(f32[32,1,16]{2,1,0:T(1,128)} %bitcast.22), calls=%async_computation.3 | async-start | bytes 32768 | tf_op jit(solution)/shard_map/all_to_all | solution.py:104
  44.0 3.0 copy-start.3
  47.0 6.2 %copy-start.4 = (f32[512,1024]{1,0:T(8,128)S(1)}, f32[512,1024]{1,0:T(8,128)}, u32[]{:S(2)}) copy-start(f32[512,1024]{1,0:T(8,128)} %get-tuple-element.21) | copy-start | bytes 6291460
  47.0 6.2 %copy-start.5 = (f32[512,1024]{1,0:T(8,128)S(1)}, f32[512,1024]{1,0:T(8,128)}, u32[]{:S(2)}) copy-start(f32[512,1024]{1,0:T(8,128)} %get-tuple-element.22) | copy-start | bytes 6291460
  146.5 4.5 %copy-start.6 = (f32[256,14,128]{2,0,1:T(8,128)S(1)}, f32[256,14,128]{2,0,1:T(8,128)}, u32[]{:S(2)}) copy-start(f32[256,14,128]{2,0,1:T(8,128)} %param.24) | copy-start | bytes 5505028
  146.5 4.5 %copy-start.11 = (f32[14,14]{1,0:T(8,128)S(1)}, f32[14,14]{1,0:T(8,128)}, u32[]{:S(2)}) copy-start(f32[14,14]{1,0:T(8,128)} %param.23) | copy-start | bytes 2356
  146.6 28.9 %all-to-all-start.1 = ((f32[8,1,57344]{2,1,0:T(1,128)}), f32[8,1,57344]{2,1,0:T(1,128)}, u32[]{:S(2)}, u32[]{:S(2)}) async-start(f32[8,1,57344]{2,1,0:T(1,128)} %reshape.131), calls=%async_computation.1 | async-start | bytes 3670016 | tf_op jit(solution)/shard_map/all_to_all | solution.py:78
  158.8 26.5 %copy-start.2 = (f32[14,8,32,128]{3,2,1,0:T(8,128)S(1)}, f32[14,8,32,128]{3,2,1,0:T(8,128)}, u32[]{:S(2)}) copy-start(f32[14,8,32,128]{3,2,1,0:T(8,128)} %param.15) | copy-start | bytes 5505028
  175.4 164.2 %all-to-all-start.2 = ((f32[32,16,14,128]{3,1,2,0:T(8,128)}), f32[32,16,14,128]{3,1,2,0:T(8,128)}, u32[]{:S(2)}, u32[]{:S(2)}) async-start(f32[32,16,14,128]{3,1,2,0:T(8,128)} %copy.61), calls=%async_computation.2 | async-start | bytes 7340032 | tf_op jit(solution)/shard_map/all_to_all | solution.py:103
  185.3 8.9 %copy-start.12 = (s32[1,2]{1,0:T(1,128)S(1)}, s32[1,2]{1,0:T(1,128)}, u32[]{:S(2)}) copy-start(s32[1,2]{1,0:T(1,128)} %param.27) | copy-start | bytes 28
  185.3 10.9 %copy-start.8 = (f32[8,32,128]{2,1,0:T(8,128)S(1)}, f32[8,32,128]{2,1,0:T(8,128)}, u32[]{:S(2)}) copy-start(f32[8,32,128]{2,1,0:T(8,128)} %param.17) | copy-start | bytes 393220
  186.3 95.1 %collective-permute-start = (f32[14,3,32,128]{3,2,1,0:T(8,128)}, f32[14,3,32,128]{3,2,1,0:T(8,128)}, u32[]{:S(2)}, u32[]{:S(2)}) collective-permute-start(f32[14,3,32,128]{3,2,1,0:T(8,128)} %get-tuple-element.19), channel_id=1, source_target_pairs={{0,8},{8,16},{16,24},{24,32},{32,40},{40,48},{48,56},{56,64},{64,7... | collective-permute-start | bytes 2064392 | tf_op jit(solution)/shard_map/ppermute | solution.py:19
  189.6 95.7 %collective-permute-start.1 = (f32[14,3,32,128]{3,2,1,0:T(8,128)S(1)}, f32[14,3,32,128]{3,2,1,0:T(8,128)S(1)}, u32[]{:S(2)}, u32[]{:S(2)}) collective-permute-start(f32[14,3,32,128]{3,2,1,0:T(8,128)S(1)} %get-tuple-element.20), channel_id=1, source_target_pairs={{8,0},{16,8},{24,16},{32,24},{40,32},{48,40},{56,48},{64,56},{72,6... | collective-permute-start | bytes 2064392 | tf_op jit(solution)/shard_map/ppermute | solution.py:20
  196.3 5.6 %copy-start.9 = (f32[8,32,128]{2,1,0:T(8,128)S(1)}, f32[8,32,128]{2,1,0:T(8,128)}, u32[]{:S(2)}) copy-start(f32[8,32,128]{2,1,0:T(8,128)} %param.16) | copy-start | bytes 393220
  196.3 5.7 %copy-start.16 = (f32[32]{0:T(128)S(1)}, f32[32]{0:T(128)}, u32[]{:S(2)}) copy-start(f32[32]{0:T(128)} %param.20) | copy-start | bytes 388
  285.4 1.6 copy-start.7
  310.8 17.1 %copy-start.14 = (f32[8,32,128]{2,1,0:T(8,128)S(1)}, f32[8,32,128]{2,1,0:T(8,128)}, u32[]{:S(2)}) copy-start(f32[8,32,128]{2,1,0:T(8,128)} %param.18) | copy-start | bytes 393220
  310.8 17.1 %copy-start.15 = (f32[14,32]{1,0:T(8,128)S(1)}, f32[14,32]{1,0:T(8,128)}, u32[]{:S(2)}) copy-start(f32[14,32]{1,0:T(8,128)} %param.22) | copy-start | bytes 5380
  310.8 17.1 %copy-start.17 = (f32[32]{0:T(128)S(1)}, f32[32]{0:T(128)}, u32[]{:S(2)}) copy-start(f32[32]{0:T(128)} %param.19) | copy-start | bytes 388
  342.1 3.1 copy-start.1
where the time goes:
time: 350 us; the launch traced here: 345 us
  waiting for transfers between devices  98.5 us (28%)
  other arithmetic  94.3 us (27%)
  local copies, waits for them, and re-layouts  76.4 us (22%)
  starting transfers between devices  38.8 us (11%)
  matrix products  36.9 us (11%)
    ppermute x1, waiting for transfers between devices, padded_2(): before = lax.ppermute(last, axis, up)  78 us
    unnamed x1, other arithmetic  66 us
    unnamed x41, local copies, waits for them, and re-layouts  30.8 us
    all_to_all x1, local copies, waits for them, and re-layouts, local(): lax.all_to_all(values, 'azim', split_axis=3, concat_axis=1, tiled=True)  17.1 us
    all_to_all x1, waiting for transfers between devices, local(): lax.all_to_all(values, 'azim', split_axis=3, concat_axis=1, tiled=True)  16.6 us
    reshape x1, local copies, waits for them, and re-layouts, local(): jnp.dot(spectrum, inverse, precision=HIGH, preferred_element_type=jnp.flo...  12.2 us
    all_to_all x1, starting transfers between devices, local(): lax.all_to_all(out_cells, 'stream', split_axis=0, concat_axis=0, tiled=True)  11.9 us
    dot_general x1, matrix products, local(): jnp.einsum('sr,rxya->sxya', net_molar_change, rate * mixed, precision=HIGH)  11.8 us
  transfers between devices with their start and end apart: 6, of which 3 were waited for; matrix products, arithmetic and copies ran while one was open for 57% of the time, Pallas kernels for 0%

commit v1 on v0

v1 whole, which is shorter than its diff:
```python
import functools
import math

import jax
import jax.numpy as jnp
import numpy as np
from jax import lax
from jax.experimental import pallas as pl
from jax.experimental.pallas import tpu as pltpu
from jax.sharding import PartitionSpec as P

STENCIL = (-1.0 / 60.0, 3.0 / 20.0, -0.75, 0.0, 0.75, -3.0 / 20.0, 1.0 / 60.0)
MESH = pl.DeviceIdType.MESH
HIGH = lax.Precision.HIGHEST
BF, F32 = jnp.bfloat16, jnp.float32

SP, CELLS, ROWS, PTS = 14, 8, 32, 128
REACT, ELEMS, BAND, GROUPS = 32, 256, 8, 8
NX, NZ, TILES = 4, 8, 32
PAD = ROWS - BAND
HALF = 16
CHUNKS = (((0, 4), (4, 8)), ((8, 11), (11, 14)))


def derivative_strip():
    points, modes = PTS * GROUPS, PTS * GROUPS // 2
    wave = np.arange(modes, dtype=np.float64)
    gain = np.where(3 * np.arange(modes) < 2 * modes, wave, 0.0)
    lag = np.arange(points)
    phase = (lag[:, None] * np.arange(modes)[None, :]) % points
    d = -2.0 / (points * modes) * (np.sin(phase * (2.0 * np.pi / points)) @ gain)
    strip = d[(lag[None, :] - np.arange(2 * PTS)[:, None]) % points].astype(np.float32)
    high = strip.astype(BF)
    low = (strip - high.astype(np.float32)).astype(BF)
    return high, low


def split(v):
    high = v.astype(BF)
    return high, (v - high.astype(F32)).astype(BF)


def dot(a, b):
    return jnp.dot(a, b, preferred_element_type=F32)


def dot3(ah, al, bh, bl):
    return dot(ah, bh) + dot(al, bh) + dot(ah, bl)


def spread(table, rows, cols):
    n, m = rows * HALF, cols * HALF
    left = (lax.broadcasted_iota(jnp.int32, (n, rows), 0) // HALF == lax.broadcasted_iota(jnp.int32, (n, rows), 1)).astype(F32).astype(BF)
    right = (lax.broadcasted_iota(jnp.int32, (cols, m), 1) // HALF == lax.broadcasted_iota(jnp.int32, (cols, m), 0)).astype(F32).astype(BF)
    same = lax.broadcasted_iota(jnp.int32, (n, m), 0) % HALF == lax.broadcasted_iota(jnp.int32, (n, m), 1) % HALF
    parts = []
    for part in split(table):
        wide = dot(dot(left, part).astype(BF), right)
        parts.append(jnp.where(same, wide, 0.0).astype(BF))
    return parts


def kernel(
    dens, axial, swirl, temp, mult, thr, cmat, nmat, tab, abl, seg, pos, bounds, strip_h, strip_l,
    out,
    dens_v, axial_v, swirl_v, temp_v, abl_v, sh_v, sl_v, kch, kcl, knh, knl, w, m3r, m3l, xr1, xl1, xal, xar, y, zr,
    fs, fr, gs, zb, halo_l, halo_r, v_wall, loc, ss, rs,
):
    s = lax.axis_index("stream")
    a = lax.axis_index("azim")
    x, z = s // NZ, lax.rem(s, NZ)
    up, down = lax.rem(s + 1, TILES), lax.rem(s + TILES - 1, TILES)
    xr, xl, xo = lax.rem(x + 1, NX), lax.rem(x + NX - 1, NX), lax.rem(x + 2, NX)
    right, left = (xr * NZ + z, a), (xl * NZ + z, a)
    y_peer = [lax.rem(a + d, GROUPS) for d in range(1, GROUPS)]
    z_peer = [lax.rem(z + d, NZ) for d in range(1, NZ)]

    barrier = pltpu.get_barrier_semaphore()
    peers = [(up, a), (down, a), right, left]
    peers += [(s, p) for p in y_peer] + [(x * NZ + p, a) for p in z_peer]
    for p in peers:
        pl.semaphore_signal(barrier, inc=1, device_id=p, device_id_type=MESH)

    local = []
    for src, dst in (
        (abl, abl_v), (dens, dens_v), (temp, temp_v), (axial, axial_v), (swirl, swirl_v),
        (strip_h, sh_v), (strip_l, sl_v),
    ):
        c = pltpu.make_async_copy(src, dst, loc.at[len(local)])
        c.start()
        local.append(c)

    count = [0]

    def remote(src, dst, device):
        n = count[0]
        count[0] += 1
        return pltpu.make_async_remote_copy(
            src_ref=src, dst_ref=dst, send_sem=ss.at[n], recv_sem=rs.at[n], device_id=device, device_id_type=MESH
        )

    target = seg[...] * CELLS + pos[...]
    place = (lax.broadcasted_iota(jnp.int32, (TILES * CELLS, ELEMS), 0) == target).astype(F32).astype(BF)
    local[0].wait()
    for p in range(SP // 2):
        block = jnp.concatenate([abl_v[2 * p], abl_v[2 * p + 1]], axis=1)
        high, low = split(block)
        sums = dot(place, high) + dot(place, low)
        w[2 * p] = sums[:, :PTS]
        w[2 * p + 1] = sums[:, PTS:]

    local[1].wait()
    start = jnp.minimum(bounds[0, 0], PAD)

    def gather(i, carry):
        for c in range(CELLS):
            fs[c, i] = dens_v[i, c, pl.ds(start, BAND), :]
        return carry

    lax.fori_loop(0, SP, gather, 0)
    pl.semaphore_wait(barrier, len(peers))

    def rows_of(block):
        return pl.ds(pl.multiple_of(block * NZ * CELLS, NZ * CELLS), NZ * CELLS)

    first, early, late = [], [], []
    for (r0, r1), (l0, l1) in CHUNKS:
        R, L = slice(r0, r1), slice(l0, l1)
        first.append([
            remote(w.at[R, rows_of(xo)], xr1.at[R], right),
            remote(w.at[L, rows_of(xo)], xl1.at[L], left),
        ])
        early.append([
            remote(w.at[L, rows_of(xr)], xal.at[L], right),
            remote(w.at[R, rows_of(xl)], xar.at[R], left),
        ])
        late.append([
            remote(m3r.at[R], xal.at[R], right),
            remote(m3l.at[L], xar.at[L], left),
        ])
    there, back = [], []
    for d in range(GROUPS - 1):
        there.append(remote(fs.at[y_peer[d]], fr.at[a], (s, y_peer[d])))
        back.append(remote(gs.at[y_peer[d]], zb.at[:, a, pl.ds(PAD, BAND)], (s, y_peer[d])))
    halo_up = remote(dens.at[:, CELLS - 3 : CELLS], halo_l, (up, a))
    halo_down = remote(dens.at[:, 0:3], halo_r, (down, a))
    z_sends = []
    for (r0, _), (_, l1) in CHUNKS:
        F = slice(r0, l1)
        z_sends.append([
            remote(y.at[F, pl.ds(pl.multiple_of(z_peer[d] * CELLS, CELLS), CELLS)], zr.at[d, F], (x * NZ + z_peer[d], a))
            for d in range(NZ - 1)
        ])

    for c in first[0] + early[0] + there:
        c.start()

    @pl.when(s < TILES - 1)
    def _():
        halo_up.start()

    @pl.when(s > 0)
    def _():
        halo_down.start()

    for c in first[1] + early[1]:
        c.start()

    fr[a] = fs[a]

    @pl.when(s == 0)
    def _():
        halo_l[...] = jnp.zeros_like(halo_l)

    @pl.when(s == TILES - 1)
    def _():
        halo_r[...] = jnp.zeros_like(halo_r)

    kch[...], kcl[...] = spread(jnp.transpose(cmat[...]), REACT, SP)
    knh[...], knl[...] = spread(nmat[...], SP, REACT)
    for c in local[2:]:
        c.wait()

    row = lax.broadcasted_iota(jnp.int32, (CELLS, ROWS, PTS), 1)
    in_band = (row >= bounds[0, 0]) & (row < bounds[0, 1])
    swirl_v[...] = jnp.where(in_band, swirl_v[...], 0.0)

    def clear(i, carry):
        zb[i, :, 0:PAD] = jnp.zeros((CELLS, PAD, PTS), F32)
        zb[i, :, PAD + BAND :] = jnp.zeros((CELLS, PAD, PTS), F32)
        return carry

    lax.fori_loop(0, SP, clear, 0)

    def chem(c, carry):
        block = dens_v[:, c]
        pair = jnp.concatenate(
            [block[:, :HALF].reshape(SP * HALF, PTS), block[:, HALF:].reshape(SP * HALF, PTS)], axis=1
        )
        high, low = split(pair)
        mixed = dot3(kch[...], kcl[...], high, low)
        minus = (-1.0 / math.log(2.0)) / temp_v[c]
        minus = jnp.concatenate([minus[:HALF], minus[HALF:]], axis=1)
        rate = jnp.concatenate([mult[q] * jnp.exp2(thr[q] * minus) for q in range(REACT)], axis=0)
        high, low = split(rate * mixed)
        made = dot3(knh[...], knl[...], high, low)
        out[:, c, 0:HALF] = made[:, :PTS].reshape(SP, HALF, PTS)
        out[:, c, HALF:] = made[:, PTS:].reshape(SP, HALF, PTS)
        return carry

    lax.fori_loop(0, 3, chem, 0)

    for k, ((r0, r1), (l0, l1)) in enumerate(CHUNKS):
        R, L = slice(r0, r1), slice(l0, l1)
        first[k][0].wait_recv()
        m3r[R] = w[R, rows_of(xr)] + xr1[R]
        late[k][0].start()
        first[k][1].wait_recv()
        m3l[L] = w[L, rows_of(xl)] + xl1[L]
        late[k][1].start()

    for c in there:
        c.wait_recv()
    lhs = jnp.concatenate(
        [
            jnp.concatenate([fr[2 * p].reshape(SP * BAND, PTS), fr[2 * p + 1].reshape(SP * BAND, PTS)], axis=1)
            for p in range(GROUPS // 2)
        ],
        axis=0,
    )
    high, low = split(lhs)
    n = SP * BAND
    shifted = [
        dot3(high, low, sh_v[:, 2 * PTS * c : 2 * PTS * (c + 1)], sl_v[:, 2 * PTS * c : 2 * PTS * (c + 1)])
        for c in range(GROUPS // 2)
    ]
    for q in range(GROUPS // 2):
        total = sum(shifted[(q - p) % 4][n * p : n * (p + 1)] for p in range(GROUPS // 2))
        gs[2 * q] = total[:, :PTS].reshape(SP, BAND, PTS)
        gs[2 * q + 1] = total[:, PTS:].reshape(SP, BAND, PTS)
    for c in back:
        c.start()
    zb[:, a, PAD : PAD + BAND] = gs[a]

    lax.fori_loop(3, 6, chem, 0)

    def finish_x(k):
        (r0, _), (_, l1) = CHUNKS[k]
        F = slice(r0, l1)
        for c in early[k] + late[k]:
            c.wait_recv()
        y[F] = w[F, rows_of(x)] + xal[F] + xar[F]
        for c in z_sends[k]:
            c.start()

    finish_x(0)
    lax.fori_loop(6, 8, chem, 0)
    finish_x(1)

    for c in back:
        c.wait_recv()

    def own(i, carry):
        f = dens_v[i]
        for c in range(CELLS):
            acc = None
            for j in (1, 2, 3):
                lo, hi = c - j >= 0, c + j < CELLS
                if lo and hi:
                    term = STENCIL[3 + j] * (f[c + j] - f[c - j])
                elif hi:
                    term = STENCIL[3 + j] * f[c + j]
                elif lo:
                    term = STENCIL[3 - j] * f[c - j]
                else:
                    continue
                acc = term if acc is None else acc + term
            around = zb[i, c, pl.ds(PAD - start, ROWS), :]
            out[i, c] = out[i, c] - axial_v[c] * acc - swirl_v[c] * around
        return carry

    lax.fori_loop(0, SP, own, 0)

    @pl.when(s > 0)
    def _():
        halo_up.wait_recv()

    @pl.when(s < TILES - 1)
    def _():
        halo_down.wait_recv()

    def ends(i, carry):
        before, after = halo_l[i], halo_r[i]
        for c in range(3):
            acc = sum(STENCIL[3 + j] * before[3 + c + j] for j in range(-3, -c))
            out[i, c] = out[i, c] - axial_v[c] * acc
            e = CELLS - 1 - c
            acc = sum(STENCIL[3 + j] * after[j - 1 - c] for j in range(c + 1, 4))
            out[i, e] = out[i, e] - axial_v[e] * acc
        return carry

    lax.fori_loop(0, SP, ends, 0)

    for k in range(len(CHUNKS)):
        for c in z_sends[k]:
            c.wait_recv()
    mine = pl.ds(pl.multiple_of(z * CELLS, CELLS), CELLS)
    for i in range(SP):
        v_wall[i] = y[i, mine] + sum(zr[d, i] for d in range(NZ - 1))
    for i in range(SP):
        wall = sum(tab[i, j] * v_wall[j] for j in range(SP))
        for c in range(CELLS):
            out[i, c, 0:1] = out[i, c, 0:1] + wall[c : c + 1]

    @pl.when(s < TILES - 1)
    def _():
        halo_up.wait_send()

    @pl.when(s > 0)
    def _():
        halo_down.wait_send()

    for group in first + early + late + z_sends + [there, back]:
        for c in group:
            c.wait_send()


def local(
    species_mass_density,
    axial_speed,
    circumferential_speed,
    thermal_kelvin_field,
    arrhenius_multiplier,
    arrhenius_threshold,
    consumed_species_orders,
    net_molar_change,
    ablated_mixture_table,
    ablator_boundary_condition,
    holding_segment,
    intra_segment_position,
    shocked_level_bounds,
):
    strip_h, strip_l = derivative_strip()
    far = pl.BlockSpec(memory_space=pltpu.HBM)
    near = pl.BlockSpec(memory_space=pltpu.VMEM)
    scalar = pl.BlockSpec(memory_space=pltpu.SMEM)
    vm = lambda shape, dtype=F32: pltpu.VMEM(shape, dtype)
    wide = NZ * CELLS
    copies = 6 * len(CHUNKS) + 2 * (GROUPS - 1) + 2 + len(CHUNKS) * (NZ - 1)
    return pl.pallas_call(
        kernel,
        name="section",
        out_shape=jax.ShapeDtypeStruct((SP, CELLS, ROWS, PTS), F32),
        in_specs=[far, far, far, far, scalar, scalar, near, near, scalar, far, near, near, scalar, far, far],
        out_specs=near,
        scratch_shapes=[
            vm((SP, CELLS, ROWS, PTS)), vm((CELLS, ROWS, PTS)), vm((CELLS, ROWS, PTS)), vm((CELLS, ROWS, PTS)),
            vm((SP, ELEMS, PTS)), vm((2 * PTS, GROUPS * PTS), BF), vm((2 * PTS, GROUPS * PTS), BF),
            vm((REACT * HALF, SP * HALF), BF), vm((REACT * HALF, SP * HALF), BF),
            vm((SP * HALF, REACT * HALF), BF), vm((SP * HALF, REACT * HALF), BF),
            vm((SP, TILES * CELLS, PTS)), vm((SP, wide, PTS)), vm((SP, wide, PTS)), vm((SP, wide, PTS)), vm((SP, wide, PTS)),
            vm((SP, wide, PTS)), vm((SP, wide, PTS)), vm((SP, wide, PTS)), vm((NZ - 1, SP, CELLS, PTS)),
            vm((GROUPS, SP, BAND, PTS)), vm((GROUPS, SP, BAND, PTS)), vm((GROUPS, SP, BAND, PTS)),
            vm((SP, CELLS, PAD + BAND + PAD, PTS)), vm((SP, 3, ROWS, PTS)), vm((SP, 3, ROWS, PTS)), vm((SP, CELLS, PTS)),
            pltpu.SemaphoreType.DMA((7,)), pltpu.SemaphoreType.DMA((copies,)), pltpu.SemaphoreType.DMA((copies,)),
        ],
        compiler_params=pltpu.CompilerParams(collective_id=0, has_side_effects=True, vmem_limit_bytes=56 << 20),
    )(
        species_mass_density, axial_speed, circumferential_speed, thermal_kelvin_field,
        arrhenius_multiplier, arrhenius_threshold, consumed_species_orders.T, net_molar_change,
        ablated_mixture_table, jnp.transpose(ablator_boundary_condition, (1, 0, 2)),
        holding_segment.reshape(1, ELEMS), intra_segment_position.reshape(1, ELEMS), shocked_level_bounds,
        jnp.asarray(strip_h), jnp.asarray(strip_l),
    )


def solution(mesh):
    in_specs = (
        P(None, "stream", None, "azim"),
        P("stream", None, "azim"),
        P("stream", None, "azim"),
        P("stream", None, "azim"),
        P(),
        P(),
        P(),
        P(),
        P(),
        P("stream", None, "azim"),
        P("stream"),
        P("stream"),
        P("stream", None),
    )
    out_specs = P(None, "stream", None, "azim")
    return jax.shard_map(local, mesh=mesh, in_specs=in_specs, out_specs=out_specs, check_vma=False)
```

time: 350 us -> 50.5 us (0.14); the launches traced: 345 us -> 49.8 us
  waiting for transfers between devices: 98.5 us -> 0 us
  other arithmetic: 94.3 us -> 0 us
  local copies, waits for them, and re-layouts: 76.4 us -> 2.9 us
  Pallas kernels: 0 us -> 46.9 us
  starting transfers between devices: 38.8 us -> 0 us
  matrix products: 36.9 us -> 0 us
    ppermute x2 -> x0, waiting for transfers between devices: 78 us -> none  [the longest x1 78 us: padded_2(): before = lax.ppermute(last, axis, up)]
    unnamed x1 -> x0, other arithmetic: 66 us -> none
    pallas_call x0 -> x1, Pallas kernels: none -> 46.9 us  [local(): pl.pallas_call(kernel, name='section', out_shape=jax.ShapeDtypeStruct((SP...]
    dot_general x8 -> x0, matrix products: 36.9 us -> none  [the longest x1 11.8 us: local(): jnp.einsum('sr,rxya->sxya', net_molar_change, rate * mixed, precision=HIGH)]
    all_to_all x4 -> x0, starting transfers between devices: 30.8 us -> none  [the longest x1 11.9 us: local(): lax.all_to_all(out_cells, 'stream', split_axis=0, concat_axis=0, tiled=True)]
    unnamed x41 -> x1, local copies, waits for them, and re-layouts: 30.8 us -> 2.9 us
    all_to_all x5 -> x0, local copies, waits for them, and re-layouts: 23.7 us -> none  [the longest x1 17.1 us: local(): lax.all_to_all(values, 'azim', split_axis=3, concat_axis=1, tiled=True)]
    all_to_all x4 -> x0, waiting for transfers between devices: 20.5 us -> none  [the longest x1 16.6 us: local(): lax.all_to_all(values, 'azim', split_axis=3, concat_axis=1, tiled=True)]
  transfers between devices with their start and end apart: 6 -> 0, of which waited for: 3 -> 0; matrix products, arithmetic and copies ran while one was open for 57% -> 0% of each run, Pallas kernels for 0% -> 0%
where the time goes in v1:
time: 50.5 us; the launch traced here: 49.8 us
  Pallas kernels  46.9 us (93%)
  local copies, waits for them, and re-layouts  2.9 us (6%)
    pallas_call x1, Pallas kernels, local(): pl.pallas_call(kernel, name='section', out_shape=jax.ShapeDtypeStruct((SP...  46.9 us
    unnamed x1, local copies, waits for them, and re-layouts  2.9 us

profile of v1, /device:TPU:2, one launch (start us, length us, event | category | flops | bytes accessed | tf_op | source)
XLA Modules:
  0.0 49.8 jit_solution(10363702452547678678)
XLA Ops:
  0.0 46.9 %section.1 = f32[14,8,32,128]{3,2,1,0:T(8,128)} custom-call(f32[14,8,32,128]{3,2,1,0:T(8,128)} %dens.1, f32[8,32,128]{2,1,0:T(8,128)} %axial.1, f32[8,32,128]{2,1,0:T(8,128)} %swirl.1, f32[8,32,128]{2,1,0:T(8,128)} %temp.1, f32[32]{0:T(128)} %mult.1, f32[32]{0:T(128)} %thr.1, f32[14,32]{1,0:T(8,128)} %bitcast.5, f32[14,32]{1,0:T(8,128)} %nmat.1, ...), custom_call_target="tpu_custom_call" | custom-call | tf_op jit(solution)/shard_map/section/pallas_call | solution.py:350
  46.9 2.9 %copy.17 = f32[14,8,32,128]{3,2,1,0:T(8,128)} copy(f32[14,8,32,128]{3,2,1,0:T(8,128)} %section.1) | data formatting | bytes 3670016

commit v2 on v1

--- a/solution.py
+++ b/solution.py
@@ -61,9 +61,9 @@
 
 
 def kernel(
-    dens, axial, swirl, temp, mult, thr, cmat, nmat, tab, abl, seg, pos, bounds, strip_h, strip_l,
+    dens, axial, swirl, temp, mult_h, thr_h, cmat_h, nmat_h, tab_h, abl, seg_h, pos_h, bounds_h, strip_h, strip_l,
     out,
-    dens_v, axial_v, swirl_v, temp_v, abl_v, sh_v, sl_v, kch, kcl, knh, knl, w, m3r, m3l, xr1, xl1, xal, xar, y, zr,
+    mult, thr, cmat, nmat, tab, seg, pos, bounds, dens_v, axial_v, swirl_v, temp_v, abl_v, sh_v, sl_v, kch, kcl, knh, knl, w, m3r, m3l, xr1, xl1, xal, xar, y, zr,
     fs, fr, gs, zb, halo_l, halo_r, v_wall, loc, ss, rs,
 ):
     s = lax.axis_index("stream")
@@ -83,8 +83,9 @@
 
     local = []
     for src, dst in (
-        (abl, abl_v), (dens, dens_v), (temp, temp_v), (axial, axial_v), (swirl, swirl_v),
-        (strip_h, sh_v), (strip_l, sl_v),
+        (seg_h, seg), (pos_h, pos), (abl, abl_v), (bounds_h, bounds), (dens, dens_v),
+        (temp, temp_v), (axial, axial_v), (swirl, swirl_v), (mult_h, mult), (thr_h, thr), (tab_h, tab),
+        (cmat_h, cmat), (nmat_h, nmat), (strip_h, sh_v), (strip_l, sl_v),
     ):
         c = pltpu.make_async_copy(src, dst, loc.at[len(local)])
         c.start()
@@ -99,9 +100,11 @@
             src_ref=src, dst_ref=dst, send_sem=ss.at[n], recv_sem=rs.at[n], device_id=device, device_id_type=MESH
         )
 
+    local[0].wait()
+    local[1].wait()
     target = seg[...] * CELLS + pos[...]
     place = (lax.broadcasted_iota(jnp.int32, (TILES * CELLS, ELEMS), 0) == target).astype(F32).astype(BF)
-    local[0].wait()
+    local[2].wait()
     for p in range(SP // 2):
         block = jnp.concatenate([abl_v[2 * p], abl_v[2 * p + 1]], axis=1)
         high, low = split(block)
@@ -109,7 +112,8 @@
         w[2 * p] = sums[:, :PTS]
         w[2 * p + 1] = sums[:, PTS:]
 
-    local[1].wait()
+    local[3].wait()
+    local[4].wait()
     start = jnp.minimum(bounds[0, 0], PAD)
 
     def gather(i, carry):
@@ -176,10 +180,10 @@
     def _():
         halo_r[...] = jnp.zeros_like(halo_r)
 
+    for c in local[5:]:
+        c.wait()
     kch[...], kcl[...] = spread(jnp.transpose(cmat[...]), REACT, SP)
     knh[...], knl[...] = spread(nmat[...], SP, REACT)
-    for c in local[2:]:
-        c.wait()
 
     row = lax.broadcasted_iota(jnp.int32, (CELLS, ROWS, PTS), 1)
     in_band = (row >= bounds[0, 0]) & (row < bounds[0, 1])
@@ -343,17 +347,20 @@
     strip_h, strip_l = derivative_strip()
     far = pl.BlockSpec(memory_space=pltpu.HBM)
     near = pl.BlockSpec(memory_space=pltpu.VMEM)
-    scalar = pl.BlockSpec(memory_space=pltpu.SMEM)
+    sm = lambda shape, dtype=F32: pltpu.SMEM(shape, dtype)
     vm = lambda shape, dtype=F32: pltpu.VMEM(shape, dtype)
     wide = NZ * CELLS
     copies = 6 * len(CHUNKS) + 2 * (GROUPS - 1) + 2 + len(CHUNKS) * (NZ - 1)
+    keep = lambda v: pltpu.with_memory_space_constraint(v, pltpu.HBM)
     return pl.pallas_call(
         kernel,
         name="section",
         out_shape=jax.ShapeDtypeStruct((SP, CELLS, ROWS, PTS), F32),
-        in_specs=[far, far, far, far, scalar, scalar, near, near, scalar, far, near, near, scalar, far, far],
+        in_specs=[far] * 15,
         out_specs=near,
         scratch_shapes=[
+            sm((REACT,)), sm((REACT,)), vm((SP, REACT)), vm((SP, REACT)), sm((SP, SP)),
+            vm((1, ELEMS), jnp.int32), vm((1, ELEMS), jnp.int32), sm((1, 2), jnp.int32),
             vm((SP, CELLS, ROWS, PTS)), vm((CELLS, ROWS, PTS)), vm((CELLS, ROWS, PTS)), vm((CELLS, ROWS, PTS)),
             vm((SP, ELEMS, PTS)), vm((2 * PTS, GROUPS * PTS), BF), vm((2 * PTS, GROUPS * PTS), BF),
             vm((REACT * HALF, SP * HALF), BF), vm((REACT * HALF, SP * HALF), BF),
@@ -362,16 +369,19 @@
             vm((SP, wide, PTS)), vm((SP, wide, PTS)), vm((SP, wide, PTS)), vm((NZ - 1, SP, CELLS, PTS)),
             vm((GROUPS, SP, BAND, PTS)), vm((GROUPS, SP, BAND, PTS)), vm((GROUPS, SP, BAND, PTS)),
             vm((SP, CELLS, PAD + BAND + PAD, PTS)), vm((SP, 3, ROWS, PTS)), vm((SP, 3, ROWS, PTS)), vm((SP, CELLS, PTS)),
-            pltpu.SemaphoreType.DMA((7,)), pltpu.SemaphoreType.DMA((copies,)), pltpu.SemaphoreType.DMA((copies,)),
+            pltpu.SemaphoreType.DMA((15,)), pltpu.SemaphoreType.DMA((copies,)), pltpu.SemaphoreType.DMA((copies,)),
         ],
-        compiler_params=pltpu.CompilerParams(collective_id=0, has_side_effects=True, vmem_limit_bytes=56 << 20),
-    )(
-        species_mass_density, axial_speed, circumferential_speed, thermal_kelvin_field,
-        arrhenius_multiplier, arrhenius_threshold, consumed_species_orders.T, net_molar_change,
-        ablated_mixture_table, jnp.transpose(ablator_boundary_condition, (1, 0, 2)),
-        holding_segment.reshape(1, ELEMS), intra_segment_position.reshape(1, ELEMS), shocked_level_bounds,
-        jnp.asarray(strip_h), jnp.asarray(strip_l),
-    )
+        compiler_params=pltpu.CompilerParams(collective_id=0, has_side_effects=True, vmem_limit_bytes=28 << 20),
+    )(*[
+        keep(v)
+        for v in (
+            species_mass_density, axial_speed, circumferential_speed, thermal_kelvin_field,
+            arrhenius_multiplier, arrhenius_threshold, consumed_species_orders.T, net_molar_change,
+            ablated_mixture_table, jnp.transpose(ablator_boundary_condition, (1, 0, 2)),
+            holding_segment.reshape(1, ELEMS), intra_segment_position.reshape(1, ELEMS), shocked_level_bounds,
+            jnp.asarray(strip_h), jnp.asarray(strip_l),
+        )
+    ])
 
 
 def solution(mesh):

time: 50.5 us -> 46.5 us (0.921)
  Pallas kernels: 46.9 us -> 44.7 us
  local copies, waits for them, and re-layouts: 2.9 us -> 1.23 us
    pallas_call x1, Pallas kernels: 46.9 us -> 44.7 us  [local(): pl.pallas_call(kernel, name='section', out_shape=jax.ShapeDtypeStruct((SP...]
    unnamed x1, local copies, waits for them, and re-layouts: 2.9 us -> 1.23 us
where the time goes in v2:
time: 46.5 us; the launch traced here: 46 us
  Pallas kernels  44.7 us (96%)
  local copies, waits for them, and re-layouts  1.23 us (3%)
    pallas_call x1, Pallas kernels, local(): pl.pallas_call(kernel, name='section', out_shape=jax.ShapeDtypeStruct((SP...  44.7 us
    unnamed x1, local copies, waits for them, and re-layouts  1.23 us

profile of v2, /device:TPU:2, one launch (start us, length us, event | category | flops | bytes accessed | tf_op | source)
XLA Modules:
  0.0 46.0 jit_solution(6703619738753337687)
XLA Ops:
  0.0 44.7 %section.1 = f32[14,8,32,128]{3,2,1,0:T(8,128)S(1)} custom-call(f32[14,8,32,128]{3,2,1,0:T(8,128)} %dens.1, f32[8,32,128]{2,1,0:T(8,128)} %axial.1, f32[8,32,128]{2,1,0:T(8,128)} %swirl.1, f32[8,32,128]{2,1,0:T(8,128)} %temp.1, f32[32]{0:T(128)} %mult_h.1, f32[32]{0:T(128)} %thr_h.1, f32[14,32]{1,0:T(8,128)} %bitcast.5, f32[14,32]{1,0:T(8,128)} %nmat_h.1, ...), custom_call_target="tpu_custom_call" | custom-call | tf_op jit(solution)/shard_map/section/pallas_call | solution.py:355
  44.8 1.2 %copy.17 = f32[14,8,32,128]{3,2,1,0:T(8,128)} copy(f32[14,8,32,128]{3,2,1,0:T(8,128)S(1)} %section.1) | data formatting | bytes 3670016

commit v3 on v2

--- a/solution.py
+++ b/solution.py
@@ -19,7 +19,8 @@
 NX, NZ, TILES = 4, 8, 32
 PAD = ROWS - BAND
 HALF = 16
-CHUNKS = (((0, 4), (4, 8)), ((8, 11), (11, 14)))
+CHUNKS = (((0, 3), (3, 6)), ((6, 8), (8, 10)), ((10, 12), (12, 14)))
+ALONG_Z, ALONG_X = (slice(0, 11),), (slice(11, 14),)
 
 
 def derivative_strip():
@@ -64,7 +65,7 @@
     dens, axial, swirl, temp, mult_h, thr_h, cmat_h, nmat_h, tab_h, abl, seg_h, pos_h, bounds_h, strip_h, strip_l,
     out,
     mult, thr, cmat, nmat, tab, seg, pos, bounds, dens_v, axial_v, swirl_v, temp_v, abl_v, sh_v, sl_v, kch, kcl, knh, knl, w, m3r, m3l, xr1, xl1, xal, xar, y, zr,
-    fs, fr, gs, zb, halo_l, halo_r, v_wall, loc, ss, rs,
+    fs, fr, gs, zb, halo_l, halo_r, turn_u, turn_d, v_wall, loc, ss, rs,
 ):
     s = lax.axis_index("stream")
     a = lax.axis_index("azim")
@@ -83,13 +84,18 @@
 
     local = []
     for src, dst in (
-        (seg_h, seg), (pos_h, pos), (abl, abl_v), (bounds_h, bounds), (dens, dens_v),
+        (seg_h, seg), (pos_h, pos), (bounds_h, bounds), (dens, dens_v),
         (temp, temp_v), (axial, axial_v), (swirl, swirl_v), (mult_h, mult), (thr_h, thr), (tab_h, tab),
         (cmat_h, cmat), (nmat_h, nmat), (strip_h, sh_v), (strip_l, sl_v),
     ):
         c = pltpu.make_async_copy(src, dst, loc.at[len(local)])
         c.start()
         local.append(c)
+    elements = []
+    for (r0, _), (_, l1) in CHUNKS:
+        c = pltpu.make_async_copy(abl.at[r0:l1], abl_v.at[r0:l1], loc.at[len(local) + len(elements)])
+        c.start()
+        elements.append(c)
 
     count = [0]
 
@@ -104,16 +110,20 @@
     local[1].wait()
     target = seg[...] * CELLS + pos[...]
     place = (lax.broadcasted_iota(jnp.int32, (TILES * CELLS, ELEMS), 0) == target).astype(F32).astype(BF)
+
+    def place_chunk(k):
+        (r0, _), (_, l1) = CHUNKS[k]
+        elements[k].wait()
+        for p in range(r0, l1, 2):
+            high, low = split(jnp.concatenate([abl_v[p], abl_v[p + 1]], axis=1))
+            sums = dot(place, high) + dot(place, low)
+            w[p] = sums[:, :PTS]
+            w[p + 1] = sums[:, PTS:]
+
+    place_chunk(0)
+
     local[2].wait()
-    for p in range(SP // 2):
-        block = jnp.concatenate([abl_v[2 * p], abl_v[2 * p + 1]], axis=1)
-        high, low = split(block)
-        sums = dot(place, high) + dot(place, low)
-        w[2 * p] = sums[:, :PTS]
-        w[2 * p + 1] = sums[:, PTS:]
-
     local[3].wait()
-    local[4].wait()
     start = jnp.minimum(bounds[0, 0], PAD)
 
     def gather(i, carry):
@@ -146,8 +156,36 @@
     for d in range(GROUPS - 1):
         there.append(remote(fs.at[y_peer[d]], fr.at[a], (s, y_peer[d])))
         back.append(remote(gs.at[y_peer[d]], zb.at[:, a, pl.ds(PAD, BAND)], (s, y_peer[d])))
-    halo_up = remote(dens.at[:, CELLS - 3 : CELLS], halo_l, (up, a))
-    halo_down = remote(dens.at[:, 0:3], halo_r, (down, a))
+    low_z, high_z, not_first, not_last = z == 0, z == NZ - 1, x > 0, x < NX - 1
+    to_low, to_high = (x * NZ, a), (x * NZ + NZ - 1, a)
+    last, begin = slice(CELLS - 3, CELLS), slice(0, 3)
+    plain, corner_zx, turn_zx, corner_xz, turn_xz = [], [], [], [], []
+    for S in ALONG_Z + ALONG_X:
+        plain.append((remote(dens.at[S, last], halo_l.at[S], (up, a)), z < NZ - 1, z > 0))
+        plain.append((remote(dens.at[S, begin], halo_r.at[S], (down, a)), z > 0, z < NZ - 1))
+    for S in ALONG_Z:
+        corner_zx.append((remote(dens.at[S, last], turn_u.at[S], to_low), high_z & not_last, low_z & not_last))
+        corner_zx.append((remote(dens.at[S, begin], turn_d.at[S], to_high), low_z & not_first, high_z & not_first))
+        turn_zx.append((remote(turn_u.at[S], halo_l.at[S], right), low_z & not_last, low_z & not_first))
+        turn_zx.append((remote(turn_d.at[S], halo_r.at[S], left), high_z & not_first, high_z & not_last))
+    for S in ALONG_X:
+        corner_xz.append((remote(dens.at[S, last], turn_u.at[S], right), high_z & not_last, high_z & not_first))
+        corner_xz.append((remote(dens.at[S, begin], turn_d.at[S], left), low_z & not_first, low_z & not_last))
+        turn_xz.append((remote(turn_u.at[S], halo_l.at[S], to_low), high_z & not_first, low_z & not_first))
+        turn_xz.append((remote(turn_d.at[S], halo_r.at[S], to_high), low_z & not_last, high_z & not_last))
+
+    def starts(group):
+        for c, sent, _ in group:
+            pl.when(sent)(c.start)
+
+    def received(group):
+        for c, _, got in group:
+            pl.when(got)(c.wait_recv)
+
+    def gone(group):
+        for c, sent, _ in group:
+            pl.when(sent)(c.wait_send)
+
     z_sends = []
     for (r0, _), (_, l1) in CHUNKS:
         F = slice(r0, l1)
@@ -156,18 +194,14 @@
             for d in range(NZ - 1)
         ])
 
-    for c in first[0] + early[0] + there:
-        c.start()
-
-    @pl.when(s < TILES - 1)
-    def _():
-        halo_up.start()
-
-    @pl.when(s > 0)
-    def _():
-        halo_down.start()
-
-    for c in first[1] + early[1]:
+    for c in first[0] + there:
+        c.start()
+    starts(plain + corner_zx)
+    place_chunk(1)
+    for c in first[1]:
+        c.start()
+    place_chunk(2)
+    for c in first[2] + early[0]:
         c.start()
 
     fr[a] = fs[a]
@@ -180,7 +214,7 @@
     def _():
         halo_r[...] = jnp.zeros_like(halo_r)
 
-    for c in local[5:]:
+    for c in local[4:]:
         c.wait()
     kch[...], kcl[...] = spread(jnp.transpose(cmat[...]), REACT, SP)
     knh[...], knl[...] = spread(nmat[...], SP, REACT)
@@ -212,9 +246,8 @@
         out[:, c, HALF:] = made[:, PTS:].reshape(SP, HALF, PTS)
         return carry
 
-    lax.fori_loop(0, 3, chem, 0)
-
-    for k, ((r0, r1), (l0, l1)) in enumerate(CHUNKS):
+    def pass_on(k):
+        (r0, r1), (l0, l1) = CHUNKS[k]
         R, L = slice(r0, r1), slice(l0, l1)
         first[k][0].wait_recv()
         m3r[R] = w[R, rows_of(xr)] + xr1[R]
@@ -222,6 +255,16 @@
         first[k][1].wait_recv()
         m3l[L] = w[L, rows_of(xl)] + xl1[L]
         late[k][1].start()
+
+    lax.fori_loop(0, 2, chem, 0)
+    pass_on(0)
+    for c in early[1]:
+        c.start()
+    lax.fori_loop(2, 3, chem, 0)
+    pass_on(1)
+    for c in early[2]:
+        c.start()
+    lax.fori_loop(3, 4, chem, 0)
 
     for c in there:
         c.wait_recv()
@@ -246,7 +289,11 @@
         c.start()
     zb[:, a, PAD : PAD + BAND] = gs[a]
 
-    lax.fori_loop(3, 6, chem, 0)
+    pass_on(2)
+    starts(corner_xz)
+    lax.fori_loop(4, 8, chem, 0)
+    received(corner_zx)
+    starts(turn_zx)
 
     def finish_x(k):
         (r0, _), (_, l1) = CHUNKS[k]
@@ -258,9 +305,7 @@
             c.start()
 
     finish_x(0)
-    lax.fori_loop(6, 8, chem, 0)
     finish_x(1)
-
     for c in back:
         c.wait_recv()
 
@@ -285,13 +330,11 @@
 
     lax.fori_loop(0, SP, own, 0)
 
-    @pl.when(s > 0)
-    def _():
-        halo_up.wait_recv()
-
-    @pl.when(s < TILES - 1)
-    def _():
-        halo_down.wait_recv()
+    finish_x(2)
+    for turned, sent in zip(corner_xz, turn_xz):
+        received([turned])
+        starts([sent])
+    received(plain + turn_zx + turn_xz)
 
     def ends(i, carry):
         before, after = halo_l[i], halo_r[i]
@@ -316,14 +359,7 @@
         for c in range(CELLS):
             out[i, c, 0:1] = out[i, c, 0:1] + wall[c : c + 1]
 
-    @pl.when(s < TILES - 1)
-    def _():
-        halo_up.wait_send()
-
-    @pl.when(s > 0)
-    def _():
-        halo_down.wait_send()
-
+    gone(plain + corner_zx + turn_zx + corner_xz + turn_xz)
     for group in first + early + late + z_sends + [there, back]:
         for c in group:
             c.wait_send()
@@ -350,7 +386,7 @@
     sm = lambda shape, dtype=F32: pltpu.SMEM(shape, dtype)
     vm = lambda shape, dtype=F32: pltpu.VMEM(shape, dtype)
     wide = NZ * CELLS
-    copies = 6 * len(CHUNKS) + 2 * (GROUPS - 1) + 2 + len(CHUNKS) * (NZ - 1)
+    copies = 6 * len(CHUNKS) + 2 * (GROUPS - 1) + 6 * len(ALONG_Z + ALONG_X) + len(CHUNKS) * (NZ - 1)
     keep = lambda v: pltpu.with_memory_space_constraint(v, pltpu.HBM)
     return pl.pallas_call(
         kernel,
@@ -368,8 +404,8 @@
             vm((SP, TILES * CELLS, PTS)), vm((SP, wide, PTS)), vm((SP, wide, PTS)), vm((SP, wide, PTS)), vm((SP, wide, PTS)),
             vm((SP, wide, PTS)), vm((SP, wide, PTS)), vm((SP, wide, PTS)), vm((NZ - 1, SP, CELLS, PTS)),
             vm((GROUPS, SP, BAND, PTS)), vm((GROUPS, SP, BAND, PTS)), vm((GROUPS, SP, BAND, PTS)),
-            vm((SP, CELLS, PAD + BAND + PAD, PTS)), vm((SP, 3, ROWS, PTS)), vm((SP, 3, ROWS, PTS)), vm((SP, CELLS, PTS)),
-            pltpu.SemaphoreType.DMA((15,)), pltpu.SemaphoreType.DMA((copies,)), pltpu.SemaphoreType.DMA((copies,)),
+            vm((SP, CELLS, PAD + BAND + PAD, PTS)), vm((SP, 3, ROWS, PTS)), vm((SP, 3, ROWS, PTS)), vm((SP, 3, ROWS, PTS)), vm((SP, 3, ROWS, PTS)), vm((SP, CELLS, PTS)),
+            pltpu.SemaphoreType.DMA((14 + len(CHUNKS),)), pltpu.SemaphoreType.DMA((copies,)), pltpu.SemaphoreType.DMA((copies,)),
         ],
         compiler_params=pltpu.CompilerParams(collective_id=0, has_side_effects=True, vmem_limit_bytes=28 << 20),
     )(*[

time: 46.5 us -> 40 us (0.86)
  Pallas kernels: 44.7 us -> 38.6 us
    pallas_call x1, Pallas kernels: 44.7 us -> 38.6 us  [local(): pl.pallas_call(kernel, name='section', out_shape=jax.ShapeDtypeStruct((SP...]
where the time goes in v3:
time: 40 us; the launch traced here: 39.9 us
  Pallas kernels  38.6 us (96%)
  local copies, waits for them, and re-layouts  1.23 us (3%)
    pallas_call x1, Pallas kernels, local(): pl.pallas_call(kernel, name='section', out_shape=jax.ShapeDtypeStruct((SP...  38.6 us
    unnamed x1, local copies, waits for them, and re-layouts  1.23 us

profile of v3, /device:TPU:2, one launch (start us, length us, event | category | flops | bytes accessed | tf_op | source)
XLA Modules:
  0.0 39.9 jit_solution(6587180898203515298)
XLA Ops:
  0.0 38.6 %section.1 = f32[14,8,32,128]{3,2,1,0:T(8,128)S(1)} custom-call(f32[14,8,32,128]{3,2,1,0:T(8,128)} %dens.1, f32[8,32,128]{2,1,0:T(8,128)} %axial.1, f32[8,32,128]{2,1,0:T(8,128)} %swirl.1, f32[8,32,128]{2,1,0:T(8,128)} %temp.1, f32[32]{0:T(128)} %mult_h.1, f32[32]{0:T(128)} %thr_h.1, f32[14,32]{1,0:T(8,128)} %bitcast.5, f32[14,32]{1,0:T(8,128)} %nmat_h.1, ...), custom_call_target="tpu_custom_call" | custom-call | tf_op jit(solution)/shard_map/section/pallas_call | solution.py:391
  38.6 1.2 %copy.17 = f32[14,8,32,128]{3,2,1,0:T(8,128)} copy(f32[14,8,32,128]{3,2,1,0:T(8,128)S(1)} %section.1) | data formatting | bytes 3670016

commit v4 on v3

--- a/solution.py
+++ b/solution.py
@@ -19,8 +19,9 @@
 NX, NZ, TILES = 4, 8, 32
 PAD = ROWS - BAND
 HALF = 16
-CHUNKS = (((0, 3), (3, 6)), ((6, 8), (8, 10)), ((10, 12), (12, 14)))
-ALONG_Z, ALONG_X = (slice(0, 11),), (slice(11, 14),)
+CHUNKS = (((0, 3), (3, 6)), ((6, 9), (9, 12)), ((12, 13), (13, 14)))
+ALONG_Z, ALONG_X = (slice(0, 4), slice(4, 8), slice(8, 11)), (slice(11, 13), slice(13, 14))
+AHEAD = 4
 
 
 def derivative_strip():
@@ -64,7 +65,7 @@
 def kernel(
     dens, axial, swirl, temp, mult_h, thr_h, cmat_h, nmat_h, tab_h, abl, seg_h, pos_h, bounds_h, strip_h, strip_l,
     out,
-    mult, thr, cmat, nmat, tab, seg, pos, bounds, dens_v, axial_v, swirl_v, temp_v, abl_v, sh_v, sl_v, kch, kcl, knh, knl, w, m3r, m3l, xr1, xl1, xal, xar, y, zr,
+    mult, thr, cmat, nmat, tab, seg, pos, bounds, dens_v, axial_v, swirl_v, temp_v, abl_v, sh_v, sl_v, kch, kcl, knh, knl, w, m3r, m3l, xr1, xl1, xal, xar, y, zr, far3, far4, two,
     fs, fr, gs, zb, halo_l, halo_r, turn_u, turn_d, v_wall, loc, ss, rs,
 ):
     s = lax.axis_index("stream")
@@ -122,16 +123,6 @@
 
     place_chunk(0)
 
-    local[2].wait()
-    local[3].wait()
-    start = jnp.minimum(bounds[0, 0], PAD)
-
-    def gather(i, carry):
-        for c in range(CELLS):
-            fs[c, i] = dens_v[i, c, pl.ds(start, BAND), :]
-        return carry
-
-    lax.fori_loop(0, SP, gather, 0)
     pl.semaphore_wait(barrier, len(peers))
 
     def rows_of(block):
@@ -186,17 +177,46 @@
         for c, sent, _ in group:
             pl.when(sent)(c.wait_send)
 
-    z_sends = []
-    for (r0, _), (_, l1) in CHUNKS:
-        F = slice(r0, l1)
-        z_sends.append([
-            remote(y.at[F, pl.ds(pl.multiple_of(z_peer[d] * CELLS, CELLS), CELLS)], zr.at[d, F], (x * NZ + z_peer[d], a))
-            for d in range(NZ - 1)
-        ])
-
-    for c in first[0] + there:
-        c.start()
-    starts(plain + corner_zx)
+    def z_to(d):
+        return (x * NZ + lax.rem(z + d + NZ, NZ), a)
+
+    def block_z(d):
+        return pl.ds(pl.multiple_of(lax.rem(z + d + NZ, NZ) * CELLS, CELLS), CELLS)
+
+    z_far, z_near, z_two = [], [], []
+    for (r0, r1), (l0, l1) in CHUNKS:
+        F, R, L = slice(r0, l1), slice(r0, r1), slice(l0, l1)
+        z_far.append([
+            remote(y.at[F, block_z(3)], far3.at[0, F], z_to(1)),
+            remote(y.at[F, block_z(-3)], far3.at[1, F], z_to(-1)),
+            remote(y.at[R, block_z(4)], far4.at[0, R], z_to(2)),
+            remote(y.at[L, block_z(4)], far4.at[1, L], z_to(-2)),
+        ])
+        z_near.append([
+            remote(y.at[F, block_z(1)], zr.at[0, F], z_to(1)),
+            remote(y.at[F, block_z(-1)], zr.at[1, F], z_to(-1)),
+        ])
+        z_two.append([
+            remote(two.at[0, F], zr.at[2, F], z_to(2)),
+            remote(two.at[1, F], zr.at[3, F], z_to(-2)),
+        ])
+
+    for c in first[0]:
+        c.start()
+    starts(corner_zx + plain[: 2 * AHEAD])
+
+    local[2].wait()
+    local[3].wait()
+    start = jnp.minimum(bounds[0, 0], PAD)
+
+    def gather(i, carry):
+        for c in range(CELLS):
+            fs[c, i] = dens_v[i, c, pl.ds(start, BAND), :]
+        return carry
+
+    lax.fori_loop(0, SP, gather, 0)
+    for c in there:
+        c.start()
     place_chunk(1)
     for c in first[1]:
         c.start()
@@ -291,9 +311,16 @@
 
     pass_on(2)
     starts(corner_xz)
-    lax.fori_loop(4, 8, chem, 0)
-    received(corner_zx)
-    starts(turn_zx)
+
+    def turn(pieces, onward, k):
+        for c, sent in zip(pieces[2 * k : 2 * k + 2], onward[2 * k : 2 * k + 2]):
+            received([c])
+            starts([sent])
+
+    turn(corner_zx, turn_zx, 0)
+    lax.fori_loop(4, 6, chem, 0)
+    turn(corner_zx, turn_zx, 1)
+    lax.fori_loop(6, 8, chem, 0)
 
     def finish_x(k):
         (r0, _), (_, l1) = CHUNKS[k]
@@ -301,11 +328,26 @@
         for c in early[k] + late[k]:
             c.wait_recv()
         y[F] = w[F, rows_of(x)] + xal[F] + xar[F]
-        for c in z_sends[k]:
+        for c in z_far[k] + z_near[k]:
             c.start()
 
+    def finish_z(k):
+        (r0, r1), (l0, l1) = CHUNKS[k]
+        for c in z_far[k]:
+            c.wait_recv()
+        two[0, r0:r1] = y[r0:r1, block_z(2)] + far3[0, r0:r1] + far4[0, r0:r1]
+        two[0, l0:l1] = y[l0:l1, block_z(2)] + far3[0, l0:l1]
+        two[1, r0:r1] = y[r0:r1, block_z(-2)] + far3[1, r0:r1]
+        two[1, l0:l1] = y[l0:l1, block_z(-2)] + far3[1, l0:l1] + far4[1, l0:l1]
+        for c in z_two[k]:
+            c.start()
+
     finish_x(0)
+    for k in range(2, len(ALONG_Z)):
+        turn(corner_zx, turn_zx, k)
+    starts(plain[2 * AHEAD :])
     finish_x(1)
+    finish_z(0)
     for c in back:
         c.wait_recv()
 
@@ -331,9 +373,10 @@
     lax.fori_loop(0, SP, own, 0)
 
     finish_x(2)
-    for turned, sent in zip(corner_xz, turn_xz):
-        received([turned])
-        starts([sent])
+    finish_z(1)
+    finish_z(2)
+    for k in range(len(ALONG_X)):
+        turn(corner_xz, turn_xz, k)
     received(plain + turn_zx + turn_xz)
 
     def ends(i, carry):
@@ -349,18 +392,18 @@
     lax.fori_loop(0, SP, ends, 0)
 
     for k in range(len(CHUNKS)):
-        for c in z_sends[k]:
+        for c in z_near[k] + z_two[k]:
             c.wait_recv()
     mine = pl.ds(pl.multiple_of(z * CELLS, CELLS), CELLS)
     for i in range(SP):
-        v_wall[i] = y[i, mine] + sum(zr[d, i] for d in range(NZ - 1))
+        v_wall[i] = y[i, mine] + sum(zr[d, i] for d in range(4))
     for i in range(SP):
         wall = sum(tab[i, j] * v_wall[j] for j in range(SP))
         for c in range(CELLS):
             out[i, c, 0:1] = out[i, c, 0:1] + wall[c : c + 1]
 
     gone(plain + corner_zx + turn_zx + corner_xz + turn_xz)
-    for group in first + early + late + z_sends + [there, back]:
+    for group in first + early + late + z_far + z_near + z_two + [there, back]:
         for c in group:
             c.wait_send()
 
@@ -386,7 +429,7 @@
     sm = lambda shape, dtype=F32: pltpu.SMEM(shape, dtype)
     vm = lambda shape, dtype=F32: pltpu.VMEM(shape, dtype)
     wide = NZ * CELLS
-    copies = 6 * len(CHUNKS) + 2 * (GROUPS - 1) + 6 * len(ALONG_Z + ALONG_X) + len(CHUNKS) * (NZ - 1)
+    copies = 6 * len(CHUNKS) + 2 * (GROUPS - 1) + 6 * len(ALONG_Z + ALONG_X) + 8 * len(CHUNKS)
     keep = lambda v: pltpu.with_memory_space_constraint(v, pltpu.HBM)
     return pl.pallas_call(
         kernel,
@@ -402,7 +445,7 @@
             vm((REACT * HALF, SP * HALF), BF), vm((REACT * HALF, SP * HALF), BF),
             vm((SP * HALF, REACT * HALF), BF), vm((SP * HALF, REACT * HALF), BF),
             vm((SP, TILES * CELLS, PTS)), vm((SP, wide, PTS)), vm((SP, wide, PTS)), vm((SP, wide, PTS)), vm((SP, wide, PTS)),
-            vm((SP, wide, PTS)), vm((SP, wide, PTS)), vm((SP, wide, PTS)), vm((NZ - 1, SP, CELLS, PTS)),
+            vm((SP, wide, PTS)), vm((SP, wide, PTS)), vm((SP, wide, PTS)), vm((4, SP, CELLS, PTS)), vm((2, SP, CELLS, PTS)), vm((2, SP, CELLS, PTS)), vm((2, SP, CELLS, PTS)),
             vm((GROUPS, SP, BAND, PTS)), vm((GROUPS, SP, BAND, PTS)), vm((GROUPS, SP, BAND, PTS)),
             vm((SP, CELLS, PAD + BAND + PAD, PTS)), vm((SP, 3, ROWS, PTS)), vm((SP, 3, ROWS, PTS)), vm((SP, 3, ROWS, PTS)), vm((SP, 3, ROWS, PTS)), vm((SP, CELLS, PTS)),
             pltpu.SemaphoreType.DMA((14 + len(CHUNKS),)), pltpu.SemaphoreType.DMA((copies,)), pltpu.SemaphoreType.DMA((copies,)),

time: 40 us -> 38.9 us (0.972)
  Pallas kernels: 38.6 us -> 37.6 us
    pallas_call x1, Pallas kernels: 38.6 us -> 37.6 us  [local(): pl.pallas_call(kernel, name='section', out_shape=jax.ShapeDtypeStruct((SP...]
where the time goes in v4:
time: 38.9 us; the launch traced here: 38.8 us
  Pallas kernels  37.6 us (97%)
  local copies, waits for them, and re-layouts  1.23 us (3%)
    pallas_call x1, Pallas kernels, local(): pl.pallas_call(kernel, name='section', out_shape=jax.ShapeDtypeStruct((SP...  37.6 us
    unnamed x1, local copies, waits for them, and re-layouts  1.23 us

profile of v4, /device:TPU:2, one launch (start us, length us, event | category | flops | bytes accessed | tf_op | source)
XLA Modules:
  0.0 38.8 jit_solution(9143359588732117447)
XLA Ops:
  0.0 37.6 %section.1 = f32[14,8,32,128]{3,2,1,0:T(8,128)S(1)} custom-call(f32[14,8,32,128]{3,2,1,0:T(8,128)} %dens.1, f32[8,32,128]{2,1,0:T(8,128)} %axial.1, f32[8,32,128]{2,1,0:T(8,128)} %swirl.1, f32[8,32,128]{2,1,0:T(8,128)} %temp.1, f32[32]{0:T(128)} %mult_h.1, f32[32]{0:T(128)} %thr_h.1, f32[14,32]{1,0:T(8,128)} %bitcast.5, f32[14,32]{1,0:T(8,128)} %nmat_h.1, ...), custom_call_target="tpu_custom_call" | custom-call | tf_op jit(solution)/shard_map/section/pallas_call | solution.py:434
  37.6 1.2 %copy.17 = f32[14,8,32,128]{3,2,1,0:T(8,128)} copy(f32[14,8,32,128]{3,2,1,0:T(8,128)S(1)} %section.1) | data formatting | bytes 3670016

commit v5 on v4

--- a/solution.py
+++ b/solution.py
@@ -20,8 +20,9 @@
 PAD = ROWS - BAND
 HALF = 16
 CHUNKS = (((0, 3), (3, 6)), ((6, 9), (9, 12)), ((12, 13), (13, 14)))
-ALONG_Z, ALONG_X = (slice(0, 4), slice(4, 8), slice(8, 11)), (slice(11, 13), slice(13, 14))
-AHEAD = 4
+ALONG_Z, ALONG_X = (slice(0, 4), slice(4, 8), slice(8, 11)), (slice(11, 12), slice(12, 13), slice(13, 14))
+EARLY_PARTS = 2
+AHEAD = 5
 
 
 def derivative_strip():
@@ -377,7 +378,6 @@
     finish_z(2)
     for k in range(len(ALONG_X)):
         turn(corner_xz, turn_xz, k)
-    received(plain + turn_zx + turn_xz)
 
     def ends(i, carry):
         before, after = halo_l[i], halo_r[i]
@@ -389,7 +389,14 @@
             out[i, e] = out[i, e] - axial_v[e] * acc
         return carry
 
-    lax.fori_loop(0, SP, ends, 0)
+    def halo_part(k):
+        onward = (turn_zx + turn_xz)[2 * k : 2 * k + 2]
+        received(plain[2 * k : 2 * k + 2] + onward)
+        S = (ALONG_Z + ALONG_X)[k]
+        lax.fori_loop(S.start, S.stop, ends, 0)
+
+    for k in range(EARLY_PARTS):
+        halo_part(k)
 
     for k in range(len(CHUNKS)):
         for c in z_near[k] + z_two[k]:
@@ -401,6 +408,10 @@
         wall = sum(tab[i, j] * v_wall[j] for j in range(SP))
         for c in range(CELLS):
             out[i, c, 0:1] = out[i, c, 0:1] + wall[c : c + 1]
+
+    for k in range(EARLY_PARTS, len(ALONG_Z + ALONG_X)):
+        halo_part(k)
+
 
     gone(plain + corner_zx + turn_zx + corner_xz + turn_xz)
     for group in first + early + late + z_far + z_near + z_two + [there, back]:

time: 38.9 us -> 38.7 us (level)
  no operation moved by 1% of the time
where the time goes in v5:
time: 38.7 us; the launch traced here: 38.6 us
  Pallas kernels  37.4 us (97%)
  local copies, waits for them, and re-layouts  1.23 us (3%)
    pallas_call x1, Pallas kernels, local(): pl.pallas_call(kernel, name='section', out_shape=jax.ShapeDtypeStruct((SP...  37.4 us
    unnamed x1, local copies, waits for them, and re-layouts  1.23 us

profile of v5, /device:TPU:2, one launch (start us, length us, event | category | flops | bytes accessed | tf_op | source)
XLA Modules:
  0.0 38.6 jit_solution(18442230671512216204)
XLA Ops:
  0.0 37.4 %section.1 = f32[14,8,32,128]{3,2,1,0:T(8,128)S(1)} custom-call(f32[14,8,32,128]{3,2,1,0:T(8,128)} %dens.1, f32[8,32,128]{2,1,0:T(8,128)} %axial.1, f32[8,32,128]{2,1,0:T(8,128)} %swirl.1, f32[8,32,128]{2,1,0:T(8,128)} %temp.1, f32[32]{0:T(128)} %mult_h.1, f32[32]{0:T(128)} %thr_h.1, f32[14,32]{1,0:T(8,128)} %bitcast.5, f32[14,32]{1,0:T(8,128)} %nmat_h.1, ...), custom_call_target="tpu_custom_call" | custom-call | tf_op jit(solution)/shard_map/section/pallas_call | solution.py:445
  37.4 1.2 %copy.17 = f32[14,8,32,128]{3,2,1,0:T(8,128)} copy(f32[14,8,32,128]{3,2,1,0:T(8,128)S(1)} %section.1) | data formatting | bytes 3670016
